TPU v7x, 32 devices: a whole 2x2x4 slice. The times are simulated.
32 devices in a mesh: grid: 4 (over y, x), day: 8 (over z, core).
Axes of the slice: x: 2, y: 2, z: 4, core: 2. Of those that a mesh axis runs over, the one named last changes fastest.
Arguments:
- anomalies: bfloat16 [8192, 16384], P('day', 'grid'), may hold values from -6 to 6
- eofs: bfloat16 [64, 16384], P(None, ('grid', 'day')), may hold values from -0.046875 to 0.046875
- means_init: float32 [8, 64], replicated, may hold values from -4 to 4
- variances: float32 [8, 64], replicated, may hold values from 0.05 to 2
- mixing: float32 [8], replicated, may hold values from 0.5 to 2
Outputs:
- regime_means: float32 [8, 64], replicated
- regime_covs: float32 [8, 64, 64], replicated
- regime_weights: float32 [8], replicated
- membership: float32 [8, 8192], P(None, 'day')
- composites: bfloat16 [8, 16384], P(None, ('grid', 'day'))
All inputs are finite; a program needn't handle non-finite values.
Results may differ from a plain program's by a relative error of at most 0.0034.
Values may be sent and summed in bfloat16 or wider, within the bound.
A program may use at most 64 MiB of HBM per device.

v0:
```python
import jax
import jax.numpy as jnp
from jax import lax
from jax.sharding import PartitionSpec as P

ITERS = 2


PRECISE = lax.Precision.HIGHEST
REG = 0.01


def log_density(pcs_t, means, covs, weights):
    regimes = means.shape[0]
    width = means.shape[1]
    eye = jnp.broadcast_to(jnp.eye(width, dtype=jnp.float32), (regimes, width, width))
    factor = jnp.linalg.cholesky(covs)
    inverse = lax.linalg.triangular_solve(factor, eye, left_side=True, lower=True)
    centred = pcs_t[None, :, :] - means[:, :, None]
    shifted = jnp.einsum("rkj,rjd->rkd", inverse, centred, precision=PRECISE)
    logdet = jnp.sum(jnp.log(jnp.diagonal(factor, axis1=1, axis2=2)), axis=1)
    return jnp.log(weights)[:, None] - logdet[:, None] - 0.5 * jnp.sum(shifted * shifted, axis=1)


def responsibilities(pcs_t, means, covs, weights):
    logp = log_density(pcs_t, means, covs, weights)
    top = jnp.max(logp, axis=0, keepdims=True)
    expo = jnp.exp(logp - top)
    return expo / jnp.sum(expo, axis=0, keepdims=True)


def second_moments(pcs_t, resp, means):
    diff = pcs_t[None, :, :] - means[:, :, None]
    return jnp.einsum("rkd,rjd->rkj", diff * resp[:, None, :], diff, precision=PRECISE)


def total_days(values):
    return lax.psum(values, "day")


def first_moments(pcs_t, resp):
    return lax.dot_general(resp, pcs_t, (((1,), (1,)), ((), ())), precision=PRECISE)


def update(pcs_t, resp, eye):
    counts, sums = total_days((jnp.sum(resp, axis=1), first_moments(pcs_t, resp)))
    counted = jnp.maximum(counts, 1.0)
    means = sums / counted[:, None]
    second = total_days(second_moments(pcs_t, resp, means))
    covs = second / counted[:, None, None] + REG * eye[None]
    weights = counted / jnp.sum(counted)
    return (means, covs, weights)


def body(anomalies, eofs, means_init, variances, mixing):
    width = eofs.shape[0]
    partial_pcs = lax.dot_general(
        anomalies,
        lax.all_gather(eofs, "day", axis=1, tiled=True),
        (((1,), (1,)), ((), ())),
        preferred_element_type=jnp.float32,
    )
    pcs = lax.psum(partial_pcs, "grid")
    pcs_t = pcs.T
    eye = jnp.eye(width, dtype=jnp.float32)
    means = means_init
    covs = variances[:, :, None] * eye[None]
    weights = mixing / jnp.sum(mixing)
    for step in range(ITERS):
        resp = responsibilities(pcs_t, means, covs, weights)
        means, covs, weights = update(pcs_t, resp, eye)
    member = responsibilities(pcs_t, means, covs, weights)
    counts = lax.psum(jnp.sum(member, axis=1), "day")
    counted = jnp.maximum(counts, 1.0)
    terms = jnp.dot(member.astype(jnp.bfloat16), anomalies, preferred_element_type=jnp.float32)
    sums = lax.psum_scatter(terms, "day", scatter_dimension=1, tiled=True)
    composites = (sums / counted[:, None]).astype(jnp.bfloat16)
    return (means, covs, weights, member, composites)


def solution(mesh):
    in_specs = (P("day", "grid"), P(None, ("grid", "day")), P(), P(), P())
    out_specs = (P(), P(), P(), P(None, "day"), P(None, ("grid", "day")))
    return jax.shard_map(body, mesh=mesh, in_specs=in_specs, out_specs=out_specs, check_vma=False)
```

profile of v0, /device:TPU:0, one launch (start us, length us, event | category | flops | bytes accessed | tf_op | source)
XLA Modules:
  0.0 503.5 jit_solution(1761515369640751929)
XLA Ops:
  7.2 16.8 %all_gather.3 = bf16[64,4096]{1,0:T(8,128)(2,1)S(1)} all-gather(bf16[64,512]{1,0:T(8,128)(2,1)} %param.9), channel_id=1, replica_groups=mesh['grid'=4,'day'=8] {'day'}, dimensions={1}, use_global_device_ids=true | all-gather | bytes 589824 | tf_op jit(solution)/shard_map/all_gather | solution.py:59
  24.0 6.8 %fusion.61 = f32[1024,64]{0,1:T(8,128)} fusion(bf16[1024,4096]{1,0:T(8,128)(2,1)} %param.8, bf16[64,4096]{1,0:T(8,128)(2,1)S(1)} %all_gather.3), kind=kOutput, calls=%fused_computation.101 | convolution fusion | flops 536870912 | bytes 9175040 | tf_op jit(solution)/shard_map/dot_general | solution.py:57
  31.1 46.9 %custom-call.16 = f32[8,64,64]{2,1,0:T(8,128)S(1)} custom-call(f32[8,64,64]{2,1,0:T(8,128)S(1)} %fusion.36), custom_call_target="Cholesky" | custom-call | tf_op jit(solution)/shard_map/jit(cholesky)/cholesky | solution.py:17
  79.0 0.9 gather_fusion
  80.5 0.7 log_subtract_fusion.2
  81.1 39.3 %custom-call.17 = f32[8,1,64,64]{2,3,1,0:T(8,128)S(1)} custom-call(f32[8,1,64,64]{3,2,1,0:T(8,128)S(1)} %get-tuple-element.33), custom_call_target="InvertDiagBlocksLowerTriangular" | custom-call | tf_op jit(solution)/shard_map/triangular_solve/custom-call.0 | solution.py:18
  121.1 3.0 multiply_reduce_fusion.2
  124.5 1.2 fusion.62
  125.7 17.2 %all-reduce.1 = (f32[8,64]{1,0:T(8,128)S(1)}, f32[8]{0:T(128)S(1)}) all-reduce(f32[8,64]{1,0:T(8,128)S(1)} %fusion.62, f32[8]{0:T(128)S(1)} %get-tuple-element.31), channel_id=1, replica_groups=mesh['grid'=4,'day'=8] {'day'}, use_global_device_ids=true, to_apply=%region_11.0 | all-reduce | flops 520 | bytes 4160 | tf_op jit(solution)/shard_map/psum | solution.py:38
  143.5 4.2 fusion.6
  148.0 53.1 %all-reduce.8.cloned.1.call-done = f32[8,64,64]{1,2,0:T(8,128)} async-done(((f32[8,64,64]{1,2,0:T(8,128)}), f32[8,64,64]{1,2,0:T(8,128)}) %all-reduce.8.cloned.1.call-update) | async-done | bytes 131088 | tf_op jit(solution)/shard_map/psum | solution.py:38
  201.0 1.0 divide_add_fusion.1
  202.2 1.1 fusion.33
  203.3 46.9 %custom-call.18 = f32[8,64,64]{2,1,0:T(8,128)S(1)} custom-call(f32[8,64,64]{2,1,0:T(8,128)S(1)} %fusion.33), custom_call_target="Cholesky" | custom-call | tf_op jit(solution)/shard_map/jit(cholesky)/cholesky | solution.py:17
  250.5 39.3 %custom-call.19 = f32[8,1,64,64]{2,3,1,0:T(8,128)S(1)} custom-call(f32[8,1,64,64]{3,2,1,0:T(8,128)S(1)} %get-tuple-element.29), custom_call_target="InvertDiagBlocksLowerTriangular" | custom-call | tf_op jit(solution)/shard_map/triangular_solve/custom-call.0 | solution.py:18
  290.4 2.0 multiply_reduce_fusion.1
  293.1 0.9 gather_fusion.1
  294.0 0.7 log_subtract_fusion.1
  295.3 14.0 %all-reduce = (f32[8,64]{1,0:T(8,128)S(1)}, f32[8]{0:T(128)S(1)}) all-reduce(f32[8,64]{1,0:T(8,128)S(1)} %fusion.63, f32[8]{0:T(128)S(1)} %get-tuple-element.27), channel_id=1, replica_groups=mesh['grid'=4,'day'=8] {'day'}, use_global_device_ids=true, to_apply=%region_17.0 | all-reduce | flops 520 | bytes 4160 | tf_op jit(solution)/shard_map/psum | solution.py:38
  310.0 3.1 fusion.2
  313.4 53.0 %all-reduce.10.cloned.1.call-done = f32[8,64,64]{1,2,0:T(8,128)} async-done(((f32[8,64,64]{1,2,0:T(8,128)}), f32[8,64,64]{1,2,0:T(8,128)}) %all-reduce.10.cloned.1.call-update) | async-done | bytes 131088 | tf_op jit(solution)/shard_map/psum | solution.py:38
  366.4 1.0 divide_add_fusion
  367.6 1.2 fusion.30
  368.8 46.9 %custom-call.20 = f32[8,64,64]{2,1,0:T(8,128)S(1)} custom-call(f32[8,64,64]{2,1,0:T(8,128)S(1)} %fusion.30), custom_call_target="Cholesky" | custom-call | tf_op jit(solution)/shard_map/jit(cholesky)/cholesky | solution.py:17
  415.9 39.3 %custom-call.21 = f32[8,1,64,64]{2,3,1,0:T(8,128)S(1)} custom-call(f32[8,1,64,64]{3,2,1,0:T(8,128)S(1)} %get-tuple-element.25), custom_call_target="InvertDiagBlocksLowerTriangular" | custom-call | tf_op jit(solution)/shard_map/triangular_solve/custom-call.0 | solution.py:18
  455.9 2.0 multiply_reduce_fusion
  458.6 0.9 gather_fusion.2
  459.5 1.2 log_subtract_fusion
  461.0 5.2 %fusion.51 = f32[8,4096]{1,0:T(8,128)} fusion(bf16[1024,4096]{1,0:T(8,128)(2,1)} %param.8, f32[8,1024]{1,0:T(8,128)S(1)} %get-tuple-element.22), kind=kOutput, calls=%fused_computation.81 | convolution fusion | flops 67117056 | bytes 8552448 | tf_op jit(solution)/shard_map/dot_general | solution.py:75
  466.3 13.7 %psum.63 = f32[8]{0:T(128)S(1)} all-reduce(f32[8]{0:T(128)S(1)} %get-tuple-element.21), channel_id=1, replica_groups=mesh['grid'=4,'day'=8] {'day'}, use_global_device_ids=true, to_apply=%region_28.31 | all-reduce | flops 8 | bytes 64 | tf_op jit(solution)/shard_map/psum | solution.py:73
  480.0 15.6 %reduce-scatter.2.cloned.1.call-done = f32[8,512]{1,0:T(8,128)} async-done(((f32[8,4096]{1,0:T(8,128)}), f32[8,512]{1,0:T(8,128)}) %reduce-scatter.2.cloned.1.call-update) | async-done | bytes 16400 | tf_op jit(solution)/shard_map/reduce_scatter | solution.py:76
  495.6 1.4 divide_convert_fusion
  (67 shorter events, 9.1 us)
Async XLA Ops:
  7.2 113.9 %all-reduce.6.cloned.1.call-start = ((), (), s32[]{:S(2)}) async-start(), calls=%async_computation.1 | async-start | bytes 524288 | tf_op jit(solution)/shard_map/psum | solution.py:63
  24.0 6.9 %copy-start.3 = (f32[8,64]{1,0:T(8,128)S(1)}, f32[8,64]{1,0:T(8,128)}, u32[]{:S(2)}) copy-start(f32[8,64]{1,0:T(8,128)} %param.11) | copy-start | bytes 6148
  30.8 170.3 %all-reduce.8.cloned.1.call-start = ((), (), s32[]{:S(2)}) async-start(), calls=%async_computation.2 | async-start | bytes 524288 | tf_op jit(solution)/shard_map/psum | solution.py:38
  31.1 48.8 %copy-start.5 = (f32[8]{0:T(128)S(1)}, f32[8]{0:T(128)}, u32[]{:S(2)}) copy-start(f32[8]{0:T(128)} %param.12) | copy-start | bytes 100
  31.1 90.0 %copy-start.6 = (f32[8,64]{1,0:T(8,128)S(1)}, f32[8,64]{1,0:T(8,128)}, u32[]{:S(2)}) copy-start(f32[8,64]{1,0:T(8,128)} %param.10) | copy-start | bytes 6148
  147.7 142.7 %copy-start = (f32[1024,64]{0,1:T(8,128)S(1)}, f32[1024,64]{0,1:T(8,128)}, u32[]{:S(2)}) copy-start(f32[1024,64]{0,1:T(8,128)} %all-reduce.6.cloned.1.call-done) | copy-start | bytes 786436
  147.7 218.7 %all-reduce.10.cloned.1.call-start = ((), (), s32[]{:S(2)}) async-start(), calls=%async_computation.3 | async-start | bytes 524288 | tf_op jit(solution)/shard_map/psum | solution.py:38
  310.0 145.9 %copy-start.4 = (f32[8,64]{1,0:T(8,128)}, f32[8,64]{1,0:T(8,128)S(1)}, u32[]{:S(2)}) copy-start(f32[8,64]{1,0:T(8,128)S(1)} %broadcast_divide_fusion) | copy-start | bytes 6148
  313.1 182.5 %reduce-scatter.2.cloned.1.call-start = ((), (), s32[]{:S(2)}) async-start(), calls=%async_computation.4 | async-start | bytes 147456 | tf_op jit(solution)/shard_map/reduce_scatter | solution.py:76
  367.6 91.0 %copy-start.1 = (f32[8,64,64]{2,1,0:T(8,128)}, f32[8,64,64]{2,1,0:T(8,128)S(1)}, u32[]{:S(2)}) copy-start(f32[8,64,64]{2,1,0:T(8,128)S(1)} %copy.27) | copy-start | bytes 393220
  461.0 5.2 %copy-start.2 = (f32[8,1024]{1,0:T(8,128)}, f32[8,1024]{1,0:T(8,128)S(1)}, u32[]{:S(2)}) copy-start(f32[8,1024]{1,0:T(8,128)S(1)} %get-tuple-element.22) | copy-start | bytes 98308
Sparse Core Ops, SparseCore 0:
  30.9 44.4 all-reduce.5
  147.9 53.1 all-reduce.7
  313.3 53.0 all-reduce.9
  466.4 29.1 reduce-scatter.1
where the time goes:
time: 504 us
  other arithmetic  271 us (54%)
  waiting for transfers between devices  122 us (24%)
  blocking collectives  61.6 us (12%)
  matrix products  29.6 us (6%)
  between operations  14.1 us (3%)
    another operation x10, other arithmetic, log_density(): factor = jnp.linalg.cholesky(covs)  141 us
    another operation x6, other arithmetic, log_density(): lax.linalg.triangular_solve(factor, eye, left_side=True, lower=True)  118 us
    psum x2, waiting for transfers between devices, total_days(): return lax.psum(values, 'day')  106 us
    psum x2, blocking collectives, total_days(): return lax.psum(values, 'day')  31.1 us
    all_gather x1, blocking collectives, body(): lax.all_gather(eofs, 'day', axis=1, tiled=True)  16.8 us
    reduce_scatter x1, waiting for transfers between devices, body(): sums = lax.psum_scatter(terms, 'day', scatter_dimension=1, tiled=True)  15.6 us
    psum x1, blocking collectives, body(): counts = lax.psum(jnp.sum(member, axis=1), 'day')  13.7 us
  transfers between devices with their start and end apart: 4, of which 3 were waited for; matrix products, arithmetic and copies ran while one was open for 18% of the time, Pallas kernels for 0%

commit v1 on v0

v1 whole, which is shorter than its diff:
```python
import functools

import jax
import jax.numpy as jnp
from jax import lax
from jax.experimental import pallas as pl
from jax.experimental.pallas import tpu as pltpu
from jax.sharding import PartitionSpec as P

ITERS = 2
REG = 0.01
MESH = pl.DeviceIdType.MESH
PRECISE = lax.Precision.HIGHEST
NT = (((1,), (1,)), ((), ()))


def columns_of(rows):
    width = rows.shape[1]
    i = lax.broadcasted_iota(jnp.int32, (width, width), 0)
    j = lax.broadcasted_iota(jnp.int32, (width, width), 1)
    eye = (i == j).astype(jnp.float32)
    return lax.dot_general(eye, rows, NT, precision=PRECISE, preferred_element_type=jnp.float32)


def softmax_regimes(logp):
    expo = jnp.exp(logp - jnp.max(logp, axis=0, keepdims=True))
    return expo / jnp.sum(expo, axis=0, keepdims=True)


def eliminate(cov):
    width = cov.shape[0]
    blocks = width // 8
    i = lax.broadcasted_iota(jnp.int32, (width, width), 0)
    j = lax.broadcasted_iota(jnp.int32, (width, width), 1)
    eye = (i == j).astype(jnp.float32)
    aug = jnp.concatenate([cov, eye], axis=1)
    rows = [aug[8 * b : 8 * b + 8, :] for b in range(blocks)]
    sub = lax.broadcasted_iota(jnp.int32, (8, 2 * width), 0)
    for step in range(width):
        b, s = step // 8, step % 8
        pivot_row = rows[b][s : s + 1, :]
        scaled = pivot_row * (1.0 / pivot_row[:, step : step + 1])
        for bb in range(b, blocks):
            column = jnp.broadcast_to(rows[bb][:, step : step + 1], (8, 2 * width))
            if bb == b:
                column = jnp.where(sub > s, column, 0.0)
            rows[bb] = rows[bb] - column * scaled
    full = jnp.concatenate(rows, axis=0)
    diag = jnp.sum(full[:, :width] * eye, axis=1, keepdims=True)
    return full * lax.rsqrt(diag), diag


def kernel(
    ng, nd, regimes, width, dl, pb,
    anom_hbm, eofs_ref, means_ref, var_ref, mix_ref,
    o_means, o_covs, o_weights, o_member, o_comp,
    anom, eall, acc, pin, msend, mrecv, gslot, res, cres, memall, csend, crecv,
    anom_sem, e_send, e_fwd, e_recv, p_send, p_recv, m_send, m_recv, g_send, g_recv,
    r_send, r_recv, c_send, c_recv, y_send, y_recv, t_send, t_recv,
):
    g = lax.axis_index("grid")
    d = lax.axis_index("day")
    half = width // 2
    sibling = d + 1 - 2 * lax.rem(d, 2)
    nz = nd // 2

    def day_peer(k):
        return lax.rem(d + k, nd)

    def grid_peer(k):
        return lax.rem(g + k, ng)

    offsets = []
    for k in range(1, nz // 2 + 1):
        offsets.append(k)
        if nz - k != k:
            offsets.append(nz - k)

    def block_pairs():
        pairs = [(d, sibling)]
        for o in offsets:
            same = lax.rem(d + 2 * o, nd)
            pairs.append((same, same + 1 - 2 * lax.rem(same, 2)))
        return pairs

    def load(s):
        return pltpu.make_async_copy(
            anom_hbm.at[:, pl.ds(pl.multiple_of(s * pb, pb), pb)], anom.at[s], anom_sem.at[s]
        )

    pairs = block_pairs()
    for pair in pairs:
        for s in pair:
            load(s).start()

    barrier = pltpu.get_barrier_semaphore()
    for k in range(1, nd):
        pl.semaphore_signal(barrier, inc=1, device_id=(g, day_peer(k)), device_id_type=MESH)
    for k in range(1, ng):
        pl.semaphore_signal(barrier, inc=1, device_id=(grid_peer(k), d), device_id_type=MESH)
    pl.semaphore_wait(barrier, nd - 1 + ng - 1)

    def remote(src, dst, send, recv, target):
        return pltpu.make_async_remote_copy(
            src_ref=src, dst_ref=dst, send_sem=send, recv_sem=recv, device_id=target, device_id_type=MESH
        )

    sent = []

    for n, target in enumerate([lax.rem(d + 2 * o, nd) for o in offsets] + [sibling]):
        copy = remote(eofs_ref, eall.at[d], e_send.at[n], e_recv.at[d], (g, target))
        copy.start()
        sent.append(copy)

    def project(s, block, i):
        days = anom[s, pl.ds(pl.multiple_of(i * dl, dl), dl), :]
        return lax.dot_general(block, days, NT, preferred_element_type=jnp.float32)

    count = 0
    for n, pair in enumerate(pairs):
        for m, s in enumerate(pair):
            if n == 0 and m == 0:
                block = eofs_ref[...]
            else:
                remote(eall.at[s], eall.at[s], e_send.at[0], e_recv.at[s], (g, sibling)).wait_recv()
                if m == 0:
                    copy = remote(eall.at[s], eall.at[s], e_fwd.at[n - 1], e_recv.at[s], (g, sibling))
                    copy.start()
                    sent.append(copy)
                block = eall[s]
            load(s).wait()
            count += 1
            if count < nd:
                first = count == 1

                def add(i, carry):
                    term = project(s, block, i)
                    acc[i] = term if first else acc[i] + term
                    return carry

                if ng <= 4:
                    for i in range(ng):
                        add(i, 0)
                else:
                    lax.fori_loop(0, ng, add, 0)
            else:
                for k in list(range(1, ng)) + [0]:
                    i = grid_peer(k)
                    total = acc[i] + project(s, block, i)
                    if k == 0:
                        pin[g] = total
                    else:
                        acc[i] = total
                        copy = remote(acc.at[i], pin.at[g], p_send.at[k - 1], p_recv.at[g], (i, d))
                        copy.start()
                        sent.append(copy)
    for k in range(1, ng):
        i = grid_peer(k)
        remote(acc.at[i], pin.at[i], p_send.at[k - 1], p_recv.at[i], (i, d)).wait_recv()
    x = pin[0]
    for i in range(1, ng):
        x = x + pin[i]

    means = means_ref[...]
    variances = var_ref[...]
    mix = mix_ref[...]
    mcol = columns_of(means)
    scale = columns_of(lax.rsqrt(variances))
    logw = jnp.log(mix / jnp.sum(mix, axis=0, keepdims=True))
    logdet = 0.5 * jnp.sum(jnp.log(variances), axis=1, keepdims=True)
    quad = []
    for r in range(regimes):
        y = (x - mcol[:, r : r + 1]) * scale[:, r : r + 1]
        quad.append(jnp.sum(y * y, axis=0, keepdims=True))
    resp = softmax_regimes(logw - logdet - 0.5 * jnp.concatenate(quad, axis=0))

    lane = lax.broadcasted_iota(jnp.int32, (8, width), 1)
    ei = lax.broadcasted_iota(jnp.int32, (width, width), 0)
    ej = lax.broadcasted_iota(jnp.int32, (width, width), 1)
    eye = (ei == ej).astype(jnp.float32)

    for it in range(ITERS):
        counts = jnp.sum(resp, axis=1, keepdims=True)
        for r in range(regimes):
            diff = x - mcol[:, r : r + 1]
            lhs = jnp.concatenate([diff * resp[r : r + 1, :], resp], axis=0)
            out = lax.dot_general(lhs, diff, NT, precision=PRECISE, preferred_element_type=jnp.float32)
            msend[it, r, 0:half, :] = jnp.concatenate([out[0:half], out[half:width]], axis=1)
            first = jnp.broadcast_to(out[width + r : width + r + 1, :], (8, width))
            number = jnp.broadcast_to(counts[r : r + 1, :], (8, width))
            msend[it, r, half : half + 8, :] = jnp.concatenate([first, number], axis=1)
            copy = remote(msend.at[it, r], mrecv.at[it, d], m_send.at[it, r], m_recv.at[it, d], (g, r))

            @pl.when(d != r)
            def _():
                copy.start()

        def own():
            mrecv[it, d] = msend[it, d]
            for k in range(1, nd):
                s = day_peer(k)
                remote(mrecv.at[it, s], mrecv.at[it, s], m_send.at[it, 0], m_recv.at[it, s], (g, s)).wait_recv()
            total = mrecv[it, 0]
            for s in range(1, nd):
                total = total + mrecv[it, s]
            gslot[it, g] = total
            for k in range(1, ng):
                copy = remote(gslot.at[it, g], gslot.at[it, g], g_send.at[it, k - 1], g_recv.at[it, g], (grid_peer(k), d))
                copy.start()
            for k in range(1, ng):
                i = grid_peer(k)
                remote(gslot.at[it, i], gslot.at[it, i], g_send.at[it, 0], g_recv.at[it, i], (i, d)).wait_recv()
            total = gslot[it, 0]
            for i in range(1, ng):
                total = total + gslot[it, i]
            second = jnp.concatenate([total[0:half, 0:width], total[0:half, width : 2 * width]], axis=0)
            first = total[half : half + 1, 0:width]
            number = total[half : half + 1, width : 2 * width]
            counted = jnp.maximum(number, 1.0)
            old = means_ref[pl.ds(d, 1), :] if it == 0 else res[it - 1, d, half : half + 1, 0:width]
            delta = (first + (number - counted) * old) / counted
            new = old + delta
            pad = jnp.zeros((6, width), jnp.float32)
            cols = columns_of(jnp.concatenate([delta, first, pad], axis=0))
            dcol, fcol = cols[:, 0:1], cols[:, 1:2]
            moved = second - dcol * first - fcol * delta + dcol * (delta * number)
            cov = moved / counted + REG * eye
            factor, diag = eliminate(cov)
            hld = 0.5 * jnp.sum(jnp.log(diag), axis=0, keepdims=True)
            res[it, d, 0:half, :] = jnp.concatenate(
                [factor[0:half, width : 2 * width], factor[half:width, width : 2 * width]], axis=1
            )
            tail = jnp.where(lane < half, jnp.broadcast_to(counted, (8, width)), jnp.broadcast_to(hld, (8, width)))
            res[it, d, half : half + 8, :] = jnp.concatenate([jnp.broadcast_to(new, (8, width)), tail], axis=1)
            for k in range(1, nd):
                remote(res.at[it, d], res.at[it, d], r_send.at[it, k - 1], r_recv.at[it, d], (g, day_peer(k))).start()
            if it == ITERS - 1:
                cres[d] = jnp.concatenate([cov[0:half], cov[half:width]], axis=1)
                for k in range(1, nd):
                    remote(cres.at[d], cres.at[d], c_send.at[k - 1], c_recv.at[d], (g, day_peer(k))).start()

        if nd > regimes:
            pl.when(d < regimes)(own)
        else:
            own()

        for r in range(regimes):
            @pl.when(d != r)
            def _():
                remote(res.at[it, r], res.at[it, r], r_send.at[it, 0], r_recv.at[it, r], (g, r)).wait_recv()

        means = jnp.concatenate([res[it, r, half : half + 1, 0:width] for r in range(regimes)], axis=0)
        tails = jnp.concatenate([res[it, r, half : half + 1, width : 2 * width] for r in range(regimes)], axis=0)
        counted = tails[:, 0:1]
        weights = counted / jnp.sum(counted, axis=0, keepdims=True)
        mcol = columns_of(means)
        quad = []
        for r in range(regimes):
            folded = res[it, r, 0:half, :]
            factor = jnp.concatenate([folded[:, 0:width], folded[:, width : 2 * width]], axis=0)
            y = jnp.dot(factor, x - mcol[:, r : r + 1], precision=PRECISE, preferred_element_type=jnp.float32)
            quad.append(jnp.sum(y * y, axis=0, keepdims=True))
        logp = jnp.log(weights) - tails[:, half : half + 1] - 0.5 * jnp.concatenate(quad, axis=0)
        resp = softmax_regimes(logp)

    memall[g] = resp
    for k in range(1, ng):
        copy = remote(memall.at[g], memall.at[g], y_send.at[k - 1], y_recv.at[g], (grid_peer(k), d))
        copy.start()
        sent.append(copy)
    o_means[...] = means
    o_weights[...] = weights
    for k in range(1, ng):
        i = grid_peer(k)
        remote(memall.at[i], memall.at[i], y_send.at[0], y_recv.at[i], (i, d)).wait_recv()
    member = jnp.concatenate([memall[i] for i in range(ng)], axis=1)
    o_member[...] = member
    counts = jnp.broadcast_to(jnp.sum(member, axis=1, keepdims=True), (regimes, 128))
    rounded = member.astype(jnp.bfloat16)

    for k in list(range(1, nd)) + [0]:
        s = day_peer(k)
        terms = jnp.dot(rounded, anom[s], preferred_element_type=jnp.float32)
        if k == 0:
            crecv[d, :, 0:pb] = terms
            crecv[d, :, pb : pb + 128] = counts
        else:
            csend[k - 1, :, 0:pb] = terms
            csend[k - 1, :, pb : pb + 128] = counts
            copy = remote(csend.at[k - 1], crecv.at[d], t_send.at[k - 1], t_recv.at[d], (g, s))
            copy.start()
            sent.append(copy)

    for r in range(regimes):
        @pl.when(d != r)
        def _():
            remote(cres.at[r], cres.at[r], c_send.at[0], c_recv.at[r], (g, r)).wait_recv()

        folded = cres[r]
        o_covs[r, 0:half, :] = folded[:, 0:width]
        o_covs[r, half:width, :] = folded[:, width : 2 * width]

    for k in range(1, nd):
        s = day_peer(k)
        remote(crecv.at[s], crecv.at[s], t_send.at[0], t_recv.at[s], (g, s)).wait_recv()
    total = crecv[0]
    for s in range(1, nd):
        total = total + crecv[s]
    o_comp[...] = (total[:, 0:pb] / jnp.maximum(total[:, pb : pb + 1], 1.0)).astype(jnp.bfloat16)

    for copy in sent:
        copy.wait_send()
    for it in range(ITERS):
        for r in range(regimes):
            @pl.when(d != r)
            def _():
                remote(msend.at[it, r], msend.at[it, r], m_send.at[it, r], m_recv.at[it, 0], (g, r)).wait_send()

        def own_sent():
            for k in range(1, ng):
                remote(gslot.at[it, g], gslot.at[it, g], g_send.at[it, k - 1], g_recv.at[it, 0], (grid_peer(k), d)).wait_send()
            for k in range(1, nd):
                remote(res.at[it, d], res.at[it, d], r_send.at[it, k - 1], r_recv.at[it, 0], (g, day_peer(k))).wait_send()
                if it == ITERS - 1:
                    remote(cres.at[d], cres.at[d], c_send.at[k - 1], c_recv.at[0], (g, day_peer(k))).wait_send()

        if nd > regimes:
            pl.when(d < regimes)(own_sent)
        else:
            own_sent()


def solution(mesh):
    ng, nd = mesh.shape["grid"], mesh.shape["day"]

    def body(anomalies, eofs, means_init, variances, mixing):
        days, pixels = anomalies.shape
        width, pb = eofs.shape
        regimes = means_init.shape[0]
        dl = days // ng
        half = width // 2
        f32 = jnp.float32
        vmem = pl.BlockSpec(memory_space=pltpu.VMEM)
        dma = pltpu.SemaphoreType.DMA
        outs = pl.pallas_call(
            functools.partial(kernel, ng, nd, regimes, width, dl, pb),
            out_shape=(
                jax.ShapeDtypeStruct((regimes, width), f32),
                jax.ShapeDtypeStruct((regimes, width, width), f32),
                jax.ShapeDtypeStruct((regimes, 1), f32),
                jax.ShapeDtypeStruct((regimes, days), f32),
                jax.ShapeDtypeStruct((regimes, pb), jnp.bfloat16),
            ),
            in_specs=[pl.BlockSpec(memory_space=pl.ANY)] + [vmem] * 4,
            out_specs=(vmem,) * 5,
            scratch_shapes=[
                pltpu.VMEM((nd, days, pb), jnp.bfloat16),
                pltpu.VMEM((nd, width, pb), jnp.bfloat16),
                pltpu.VMEM((ng, width, dl), f32),
                pltpu.VMEM((ng, width, dl), f32),
                pltpu.VMEM((ITERS, regimes, half + 8, 2 * width), f32),
                pltpu.VMEM((ITERS, nd, half + 8, 2 * width), f32),
                pltpu.VMEM((ITERS, ng, half + 8, 2 * width), f32),
                pltpu.VMEM((ITERS, regimes, half + 8, 2 * width), f32),
                pltpu.VMEM((regimes, half, 2 * width), f32),
                pltpu.VMEM((ng, regimes, dl), f32),
                pltpu.VMEM((nd - 1, regimes, pb + 128), f32),
                pltpu.VMEM((nd, regimes, pb + 128), f32),
                dma((nd,)),
                dma((nd // 2,)),
                dma((nd // 2,)),
                dma((nd,)),
                dma((ng,)),
                dma((ng,)),
                dma((ITERS, regimes)),
                dma((ITERS, nd)),
                dma((ITERS, ng)),
                dma((ITERS, ng)),
                dma((ITERS, nd)),
                dma((ITERS, regimes)),
                dma((nd,)),
                dma((regimes,)),
                dma((ng,)),
                dma((ng,)),
                dma((nd,)),
                dma((nd,)),
            ],
            compiler_params=pltpu.CompilerParams(
                collective_id=0, has_side_effects=True, vmem_limit_bytes=40 * 1024 * 1024
            ),
            name="regimes",
        )(anomalies, eofs, means_init, variances, mixing.reshape(regimes, 1))
        means, covs, weights, member, comp = outs
        return means, covs, weights.reshape(regimes), member, comp

    in_specs = (P("day", "grid"), P(None, ("grid", "day")), P(), P(), P())
    out_specs = (P(), P(), P(), P(None, "day"), P(None, ("grid", "day")))
    return jax.shard_map(body, mesh=mesh, in_specs=in_specs, out_specs=out_specs, check_vma=False)
```

time: 504 us -> 83.5 us (0.17)
  other arithmetic: 271 us -> 0.63 us
  waiting for transfers between devices: 122 us -> 0 us
  Pallas kernels: 0 us -> 73.2 us
  blocking collectives: 61.6 us -> 0 us
  matrix products: 29.6 us -> 0 us
  between operations: 14.1 us -> 0.65 us
    another operation x16 -> x0, other arithmetic: 259 us -> none  [the longest x10 141 us: log_density(): factor = jnp.linalg.cholesky(covs)]
    psum x3 -> x0, waiting for transfers between devices: 106 us -> none  [the longest x2 106 us: total_days(): return lax.psum(values, 'day')]
    pallas_call x0 -> x1, Pallas kernels: none -> 73.2 us  [body(): pl.pallas_call(functools.partial(kernel, ng, nd, regimes, width, dl, pb),...]
    psum x3 -> x0, blocking collectives: 44.8 us -> none  [the longest x2 31.1 us: total_days(): return lax.psum(values, 'day')]
    dot_general x9 -> x0, matrix products: 27.8 us -> none  [the longest x2 7.29 us: second_moments(): jnp.einsum('rkd,rjd->rkj', diff * resp[:, None, :], diff, precision=PRECISE)]
    all_gather x1 -> x0, blocking collectives: 16.8 us -> none  [body(): lax.all_gather(eofs, 'day', axis=1, tiled=True)]
    reduce_scatter x1 -> x0, waiting for transfers between devices: 15.6 us -> none  [body(): sums = lax.psum_scatter(terms, 'day', scatter_dimension=1, tiled=True)]
    unnamed x15 -> x12, local copies, waits for them, and re-layouts: 0.16 us -> 8.1 us
  transfers between devices with their start and end apart: 4 -> 0, of which waited for: 3 -> 0; matrix products, arithmetic and copies ran while one was open for 18% -> 0% of each run, Pallas kernels for 0% -> 0%
where the time goes in v1:
time: 83.5 us; the launch traced here: 83.3 us
  Pallas kernels  73.2 us (88%)
  local copies, waits for them, and re-layouts  8.83 us (11%)
    pallas_call x1, Pallas kernels, body(): pl.pallas_call(functools.partial(kernel, ng, nd, regimes, width, dl, pb),...  73.2 us
    unnamed x12, local copies, waits for them, and re-layouts  8.1 us

profile of v1, /device:TPU:0, one launch (start us, length us, event | category | flops | bytes accessed | tf_op | source)
XLA Modules:
  0.0 83.3 jit_solution(16159343838071219784)
XLA Ops:
  0.6 0.7 copy.11.mix_ref
  1.4 0.0 copy-start
  1.4 3.4 %copy-done = bf16[1024,4096]{1,0:T(8,128)(2,1)S(1)} copy-done((bf16[1024,4096]{1,0:T(8,128)(2,1)S(1)}, bf16[1024,4096]{1,0:T(8,128)(2,1)}, u32[]{:S(2)}) %copy-start) | copy-done | bytes 8388632
  4.7 0.0 copy-start.1
  4.7 0.8 %copy-done.1 = bf16[64,512]{1,0:T(8,128)(2,1)S(1)} copy-done((bf16[64,512]{1,0:T(8,128)(2,1)S(1)}, bf16[64,512]{1,0:T(8,128)(2,1)}, u32[]{:S(2)}) %copy-start.1) | copy-done | bytes 65560
  5.6 0.0 copy-start.2
  5.6 0.7 copy-done.2
  6.3 0.0 copy-start.3
  6.3 0.7 copy-done.3
  7.0 73.2 %regimes.1 = (f32[8,64]{1,0:T(8,128)S(1)}, f32[8,64,64]{2,1,0:T(8,128)S(1)}, f32[8,1]{1,0:T(8,128)S(1)}, f32[8,1024]{1,0:T(8,128)S(1)}, bf16[8,512]{1,0:T(8,128)(2,1)S(1)}) custom-call(bf16[1024,4096]{1,0:T(8,128)(2,1)S(1)} %copy-done, bf16[64,512]{1,0:T(8,128)(2,1)S(1)} %copy-done.1, f32[8,64]{1,0:T(8,128)S(1)} %copy-done.2, f32[8,64]{1,0:T(8,128)S(1)} %copy-done.3, ...), custom_call_target="tpu_custom_call" | custom-call | tf_op jit(solution)/shard_map/regimes/pallas_call | solution.py:345
  80.1 0.6 reduce
  80.7 0.6 copy.16
  81.3 0.7 copy.17
  82.0 0.6 copy.18
  82.7 0.6 copy.19
Async XLA Ops:
  1.4 3.4 %copy-start = (bf16[1024,4096]{1,0:T(8,128)(2,1)S(1)}, bf16[1024,4096]{1,0:T(8,128)(2,1)}, u32[]{:S(2)}) copy-start(bf16[1024,4096]{1,0:T(8,128)(2,1)} %anom_hbm.1) | copy-start | bytes 25165828
  4.7 0.8 %copy-start.1 = (bf16[64,512]{1,0:T(8,128)(2,1)S(1)}, bf16[64,512]{1,0:T(8,128)(2,1)}, u32[]{:S(2)}) copy-start(bf16[64,512]{1,0:T(8,128)(2,1)} %eofs_ref.1) | copy-start | bytes 196612
  5.6 0.7 copy-start.2
  6.3 0.7 copy-start.3

commit v2 on v1

--- a/solution.py
+++ b/solution.py
@@ -35,16 +35,25 @@
     eye = (i == j).astype(jnp.float32)
     aug = jnp.concatenate([cov, eye], axis=1)
     rows = [aug[8 * b : 8 * b + 8, :] for b in range(blocks)]
-    sub = lax.broadcasted_iota(jnp.int32, (8, 2 * width), 0)
-    for step in range(width):
-        b, s = step // 8, step % 8
-        pivot_row = rows[b][s : s + 1, :]
-        scaled = pivot_row * (1.0 / pivot_row[:, step : step + 1])
-        for bb in range(b, blocks):
-            column = jnp.broadcast_to(rows[bb][:, step : step + 1], (8, 2 * width))
-            if bb == b:
-                column = jnp.where(sub > s, column, 0.0)
-            rows[bb] = rows[bb] - column * scaled
+    wide = (8, 2 * width)
+    sub = lax.broadcasted_iota(jnp.int32, wide, 0)
+    for b in range(blocks):
+        cols = [
+            [jnp.broadcast_to(rows[bb][:, 8 * b + k : 8 * b + k + 1], wide) for bb in range(b, blocks)]
+            for k in range(8)
+        ]
+        for s in range(8):
+            inverse = 1.0 / jnp.broadcast_to(cols[s][0][s : s + 1, :], wide)
+            pivot_row = jnp.broadcast_to(rows[b][s : s + 1, :], wide)
+            later = [jnp.broadcast_to(cols[k][0][s : s + 1, :], wide) for k in range(s + 1, 8)]
+            for n in range(blocks - b):
+                column = cols[s][n]
+                if n == 0:
+                    column = jnp.where(sub > s, column, 0.0)
+                factor = column * inverse
+                for k in range(s + 1, 8):
+                    cols[k][n] = cols[k][n] - factor * later[k - s - 1]
+                rows[b + n] = rows[b + n] - factor * pivot_row
     full = jnp.concatenate(rows, axis=0)
     diag = jnp.sum(full[:, :width] * eye, axis=1, keepdims=True)
     return full * lax.rsqrt(diag), diag
@@ -52,11 +61,11 @@
 
 def kernel(
     ng, nd, regimes, width, dl, pb,
-    anom_hbm, eofs_ref, means_ref, var_ref, mix_ref,
+    anom_hbm, eofs_ref, means_hbm, var_hbm, mix_hbm,
     o_means, o_covs, o_weights, o_member, o_comp,
-    anom, eall, acc, pin, msend, mrecv, gslot, res, cres, memall, csend, crecv,
+    means_ref, var_ref, mix_ref, anom, eall, acc, pin, msend, mrecv, gslot, res, cres, memall, csend, crecv,
     anom_sem, e_send, e_fwd, e_recv, p_send, p_recv, m_send, m_recv, g_send, g_recv,
-    r_send, r_recv, c_send, c_recv, y_send, y_recv, t_send, t_recv,
+    r_send, r_recv, c_send, c_recv, y_send, y_recv, t_send, t_recv, i_sem,
 ):
     g = lax.axis_index("grid")
     d = lax.axis_index("day")
@@ -88,6 +97,14 @@
             anom_hbm.at[:, pl.ds(pl.multiple_of(s * pb, pb), pb)], anom.at[s], anom_sem.at[s]
         )
 
+    first_copies = [
+        pltpu.make_async_copy(eofs_ref, eall.at[d], i_sem.at[0]),
+        pltpu.make_async_copy(means_hbm, means_ref, i_sem.at[1]),
+        pltpu.make_async_copy(var_hbm, var_ref, i_sem.at[2]),
+        pltpu.make_async_copy(mix_hbm, mix_ref, i_sem.at[3]),
+    ]
+    for copy in first_copies:
+        copy.start()
     pairs = block_pairs()
     for pair in pairs:
         for s in pair:
@@ -120,7 +137,8 @@
     for n, pair in enumerate(pairs):
         for m, s in enumerate(pair):
             if n == 0 and m == 0:
-                block = eofs_ref[...]
+                first_copies[0].wait()
+                block = eall[s]
             else:
                 remote(eall.at[s], eall.at[s], e_send.at[0], e_recv.at[s], (g, sibling)).wait_recv()
                 if m == 0:
@@ -161,9 +179,13 @@
     for i in range(1, ng):
         x = x + pin[i]
 
+    for copy in first_copies[1:]:
+        copy.wait()
     means = means_ref[...]
     variances = var_ref[...]
-    mix = mix_ref[...]
+    er = lax.broadcasted_iota(jnp.int32, (regimes, regimes), 0)
+    ec = lax.broadcasted_iota(jnp.int32, (regimes, regimes), 1)
+    mix = jnp.sum(jnp.where(er == ec, mix_ref[...].reshape(1, regimes), 0.0), axis=1, keepdims=True)
     mcol = columns_of(means)
     scale = columns_of(lax.rsqrt(variances))
     logw = jnp.log(mix / jnp.sum(mix, axis=0, keepdims=True))
@@ -269,7 +291,7 @@
         copy.start()
         sent.append(copy)
     o_means[...] = means
-    o_weights[...] = weights
+    o_weights[...] = jnp.sum(jnp.where(er == ec, weights, 0.0), axis=0)
     for k in range(1, ng):
         i = grid_peer(k)
         remote(memall.at[i], memall.at[i], y_send.at[0], y_recv.at[i], (i, d)).wait_recv()
@@ -347,13 +369,16 @@
             out_shape=(
                 jax.ShapeDtypeStruct((regimes, width), f32),
                 jax.ShapeDtypeStruct((regimes, width, width), f32),
-                jax.ShapeDtypeStruct((regimes, 1), f32),
+                jax.ShapeDtypeStruct((regimes,), f32),
                 jax.ShapeDtypeStruct((regimes, days), f32),
                 jax.ShapeDtypeStruct((regimes, pb), jnp.bfloat16),
             ),
-            in_specs=[pl.BlockSpec(memory_space=pl.ANY)] + [vmem] * 4,
+            in_specs=[pl.BlockSpec(memory_space=pltpu.HBM)] * 5,
             out_specs=(vmem,) * 5,
             scratch_shapes=[
+                pltpu.VMEM((regimes, width), f32),
+                pltpu.VMEM((regimes, width), f32),
+                pltpu.VMEM((regimes,), f32),
                 pltpu.VMEM((nd, days, pb), jnp.bfloat16),
                 pltpu.VMEM((nd, width, pb), jnp.bfloat16),
                 pltpu.VMEM((ng, width, dl), f32),
@@ -384,14 +409,14 @@
                 dma((ng,)),
                 dma((nd,)),
                 dma((nd,)),
+                dma((4,)),
             ],
             compiler_params=pltpu.CompilerParams(
-                collective_id=0, has_side_effects=True, vmem_limit_bytes=40 * 1024 * 1024
+                collective_id=0, has_side_effects=True, vmem_limit_bytes=48 * 1024 * 1024
             ),
             name="regimes",
-        )(anomalies, eofs, means_init, variances, mixing.reshape(regimes, 1))
-        means, covs, weights, member, comp = outs
-        return means, covs, weights.reshape(regimes), member, comp
+        )(anomalies, eofs, means_init, variances, mixing)
+        return outs
 
     in_specs = (P("day", "grid"), P(None, ("grid", "day")), P(), P(), P())
     out_specs = (P(), P(), P(), P(None, "day"), P(None, ("grid", "day")))

time: 83.5 us -> 71.6 us (0.86)
  Pallas kernels: 73.2 us -> 64.9 us
  local copies, waits for them, and re-layouts: 8.83 us -> 5.88 us
    pallas_call x1, Pallas kernels: 73.2 us -> 64.9 us  [body(): pl.pallas_call(functools.partial(kernel, ng, nd, regimes, width, dl, pb),...]
    unnamed x12 -> x13, local copies, waits for them, and re-layouts: 8.1 us -> 5.88 us
where the time goes in v2:
time: 71.6 us; the launch traced here: 71.4 us
  Pallas kernels  64.9 us (91%)
  local copies, waits for them, and re-layouts  5.88 us (8%)
    pallas_call x1, Pallas kernels, body(): pl.pallas_call(functools.partial(kernel, ng, nd, regimes, width, dl, pb),...  64.9 us
    unnamed x13, local copies, waits for them, and re-layouts  5.88 us

profile of v2, /device:TPU:0, one launch (start us, length us, event | category | flops | bytes accessed | tf_op | source)
XLA Modules:
  0.0 71.4 jit_solution(12109287786893434301)
XLA Ops:
  0.6 0.0 copy-start
  0.6 0.8 %copy-done = bf16[64,512]{1,0:T(8,128)(2,1)S(1)} copy-done((bf16[64,512]{1,0:T(8,128)(2,1)S(1)}, bf16[64,512]{1,0:T(8,128)(2,1)}, u32[]{:S(2)}) %copy-start) | copy-done | bytes 65560
  1.5 0.0 copy-start.1
  1.5 0.7 copy-done.1
  2.2 0.0 copy-start.2
  2.2 0.7 copy-done.2
  2.8 0.0 copy-start.3
  2.9 0.7 copy-done.3
  3.5 64.9 %regimes.1 = (f32[8,64]{1,0:T(8,128)S(1)}, f32[8,64,64]{2,1,0:T(8,128)S(1)}, f32[8]{0:T(128)S(1)}, f32[8,1024]{1,0:T(8,128)S(1)}, bf16[8,512]{1,0:T(8,128)(2,1)S(1)}) custom-call(bf16[1024,4096]{1,0:T(8,128)(2,1)} %anom_hbm.1, bf16[64,512]{1,0:T(8,128)(2,1)S(1)} %copy-done, f32[8,64]{1,0:T(8,128)S(1)} %copy-done.1, f32[8,64]{1,0:T(8,128)S(1)} %copy-done.2, ...), custom_call_target="tpu_custom_call" | custom-call | tf_op jit(solution)/shard_map/regimes/pallas_call | solution.py:367
  68.4 0.6 copy.15
  69.0 0.7 copy.16
  69.7 0.5 copy.17
  70.2 0.6 copy.18
  70.8 0.6 copy.19
Async XLA Ops:
  0.6 0.8 %copy-start = (bf16[64,512]{1,0:T(8,128)(2,1)S(1)}, bf16[64,512]{1,0:T(8,128)(2,1)}, u32[]{:S(2)}) copy-start(bf16[64,512]{1,0:T(8,128)(2,1)} %eofs_ref.1) | copy-start | bytes 196612
  1.5 0.7 copy-start.1
  2.2 0.7 copy-start.2
  2.8 0.7 copy-start.3

commit v3 on v2

--- a/solution.py
+++ b/solution.py
@@ -63,15 +63,18 @@
     ng, nd, regimes, width, dl, pb,
     anom_hbm, eofs_ref, means_hbm, var_hbm, mix_hbm,
     o_means, o_covs, o_weights, o_member, o_comp,
-    means_ref, var_ref, mix_ref, anom, eall, acc, pin, msend, mrecv, gslot, res, cres, memall, csend, crecv,
-    anom_sem, e_send, e_fwd, e_recv, p_send, p_recv, m_send, m_recv, g_send, g_recv,
-    r_send, r_recv, c_send, c_recv, y_send, y_recv, t_send, t_recv, i_sem,
+    means_ref, var_ref, mix_ref, anom, eall, acc, pin, msend, msib, chip, mrecv, gslot, res, cres, memall, cout, cin, csend, crecv, cnt,
+    anom_sem, e_send, e_fwd, e_recv, p_send, p_recv, s_send, s_recv, m_send, m_recv, g_send, g_recv,
+    r_send, r_fwd, r_recv, c_send, c_fwd, c_recv, y_send, y_recv, u_send, u_recv, t_send, t_recv, n_send, n_recv, i_sem,
 ):
     g = lax.axis_index("grid")
     d = lax.axis_index("day")
     half = width // 2
     sibling = d + 1 - 2 * lax.rem(d, 2)
     nz = nd // 2
+    pairs_of = regimes // 2
+    core = lax.rem(d, 2)
+    z = lax.div(d, 2)
 
     def day_peer(k):
         return lax.rem(d + k, nd)
@@ -124,7 +127,8 @@
 
     sent = []
 
-    for n, target in enumerate([lax.rem(d + 2 * o, nd) for o in offsets] + [sibling]):
+    near = [lax.rem(d + 2 * o, nd) for o in offsets] + [sibling]
+    for n, target in enumerate(near):
         copy = remote(eofs_ref, eall.at[d], e_send.at[n], e_recv.at[d], (g, target))
         copy.start()
         sent.append(copy)
@@ -211,19 +215,27 @@
             first = jnp.broadcast_to(out[width + r : width + r + 1, :], (8, width))
             number = jnp.broadcast_to(counts[r : r + 1, :], (8, width))
             msend[it, r, half : half + 8, :] = jnp.concatenate([first, number], axis=1)
-            copy = remote(msend.at[it, r], mrecv.at[it, d], m_send.at[it, r], m_recv.at[it, d], (g, r))
-
-            @pl.when(d != r)
+
+            @pl.when(core != r % 2)
             def _():
-                copy.start()
+                remote(msend.at[it, r], msib.at[it, r // 2], s_send.at[it, r // 2], s_recv.at[it, r // 2], (g, sibling)).start()
+
+        for n in range(pairs_of):
+            mine = 2 * n + core
+            remote(msib.at[it, n], msib.at[it, n], s_send.at[it, n], s_recv.at[it, n], (g, sibling)).wait_recv()
+            chip[it, n] = msend[it, mine] + msib[it, n]
+
+            @pl.when(z != n)
+            def _():
+                remote(chip.at[it, n], mrecv.at[it, z], m_send.at[it, n], m_recv.at[it, z], (g, mine)).start()
 
         def own():
-            mrecv[it, d] = msend[it, d]
-            for k in range(1, nd):
-                s = day_peer(k)
-                remote(mrecv.at[it, s], mrecv.at[it, s], m_send.at[it, 0], m_recv.at[it, s], (g, s)).wait_recv()
+            mrecv[it, z] = chip[it, z]
+            for k in range(1, nz):
+                s = lax.rem(z + k, nz)
+                remote(mrecv.at[it, s], mrecv.at[it, s], m_send.at[it, 0], m_recv.at[it, s], (g, sibling)).wait_recv()
             total = mrecv[it, 0]
-            for s in range(1, nd):
+            for s in range(1, nz):
                 total = total + mrecv[it, s]
             gslot[it, g] = total
             for k in range(1, ng):
@@ -254,22 +266,30 @@
             )
             tail = jnp.where(lane < half, jnp.broadcast_to(counted, (8, width)), jnp.broadcast_to(hld, (8, width)))
             res[it, d, half : half + 8, :] = jnp.concatenate([jnp.broadcast_to(new, (8, width)), tail], axis=1)
-            for k in range(1, nd):
-                remote(res.at[it, d], res.at[it, d], r_send.at[it, k - 1], r_recv.at[it, d], (g, day_peer(k))).start()
+            for n, target in enumerate(near):
+                remote(res.at[it, d], res.at[it, d], r_send.at[it, n], r_recv.at[it, d], (g, target)).start()
             if it == ITERS - 1:
                 cres[d] = jnp.concatenate([cov[0:half], cov[half:width]], axis=1)
-                for k in range(1, nd):
-                    remote(cres.at[d], cres.at[d], c_send.at[k - 1], c_recv.at[d], (g, day_peer(k))).start()
+                for n, target in enumerate(near):
+                    remote(cres.at[d], cres.at[d], c_send.at[n], c_recv.at[d], (g, target)).start()
 
         if nd > regimes:
             pl.when(d < regimes)(own)
         else:
             own()
 
-        for r in range(regimes):
-            @pl.when(d != r)
+        for n in range(pairs_of):
+            r = 2 * n + core
+
+            @pl.when(z != n)
             def _():
-                remote(res.at[it, r], res.at[it, r], r_send.at[it, 0], r_recv.at[it, r], (g, r)).wait_recv()
+                copy = remote(res.at[it, r], res.at[it, r], r_fwd.at[it, n], r_recv.at[it, r], (g, sibling))
+                copy.wait_recv()
+                copy.start()
+
+        for n in range(pairs_of):
+            r = 2 * n + 1 - core
+            remote(res.at[it, r], res.at[it, r], r_fwd.at[it, n], r_recv.at[it, r], (g, sibling)).wait_recv()
 
         means = jnp.concatenate([res[it, r, half : half + 1, 0:width] for r in range(regimes)], axis=0)
         tails = jnp.concatenate([res[it, r, half : half + 1, width : 2 * width] for r in range(regimes)], axis=0)
@@ -297,59 +317,97 @@
         remote(memall.at[i], memall.at[i], y_send.at[0], y_recv.at[i], (i, d)).wait_recv()
     member = jnp.concatenate([memall[i] for i in range(ng)], axis=1)
     o_member[...] = member
-    counts = jnp.broadcast_to(jnp.sum(member, axis=1, keepdims=True), (regimes, 128))
+    cnt[d] = jnp.broadcast_to(jnp.sum(member, axis=1, keepdims=True), (regimes, 128))
+    for k in range(1, nd):
+        copy = remote(cnt.at[d], cnt.at[d], n_send.at[k - 1], n_recv.at[d], (g, day_peer(k)))
+        copy.start()
+        sent.append(copy)
     rounded = member.astype(jnp.bfloat16)
 
-    for k in list(range(1, nd)) + [0]:
-        s = day_peer(k)
-        terms = jnp.dot(rounded, anom[s], preferred_element_type=jnp.float32)
-        if k == 0:
-            crecv[d, :, 0:pb] = terms
-            crecv[d, :, pb : pb + 128] = counts
+    order = [lax.rem(z + o, nz) for o in reversed(offsets)] + [z]
+    for n in order:
+        cout[n] = jnp.dot(rounded, anom[2 * n + 1 - core], preferred_element_type=jnp.float32)
+        copy = remote(cout.at[n], cin.at[n], u_send.at[n], u_recv.at[n], (g, sibling))
+        copy.start()
+        sent.append(copy)
+
+    for n in range(pairs_of):
+        r = 2 * n + core
+
+        @pl.when(z != n)
+        def _():
+            copy = remote(cres.at[r], cres.at[r], c_fwd.at[n], c_recv.at[r], (g, sibling))
+            copy.wait_recv()
+            copy.start()
+
+    for n in order:
+        terms = jnp.dot(rounded, anom[2 * n + core], preferred_element_type=jnp.float32)
+        remote(cin.at[n], cin.at[n], u_send.at[n], u_recv.at[n], (g, sibling)).wait_recv()
+        terms = terms + cin[n]
+        if n is z:
+            crecv[z] = terms
         else:
-            csend[k - 1, :, 0:pb] = terms
-            csend[k - 1, :, pb : pb + 128] = counts
-            copy = remote(csend.at[k - 1], crecv.at[d], t_send.at[k - 1], t_recv.at[d], (g, s))
+            csend[n] = terms
+            copy = remote(csend.at[n], crecv.at[z], t_send.at[n], t_recv.at[z], (g, 2 * n + core))
             copy.start()
             sent.append(copy)
 
+    for n in range(pairs_of):
+        r = 2 * n + 1 - core
+        remote(cres.at[r], cres.at[r], c_fwd.at[n], c_recv.at[r], (g, sibling)).wait_recv()
     for r in range(regimes):
-        @pl.when(d != r)
-        def _():
-            remote(cres.at[r], cres.at[r], c_send.at[0], c_recv.at[r], (g, r)).wait_recv()
-
         folded = cres[r]
         o_covs[r, 0:half, :] = folded[:, 0:width]
         o_covs[r, half:width, :] = folded[:, width : 2 * width]
 
     for k in range(1, nd):
         s = day_peer(k)
-        remote(crecv.at[s], crecv.at[s], t_send.at[0], t_recv.at[s], (g, s)).wait_recv()
+        remote(cnt.at[s], cnt.at[s], n_send.at[0], n_recv.at[s], (g, s)).wait_recv()
+    number = cnt[0]
+    for s in range(1, nd):
+        number = number + cnt[s]
+    for n in order[:-1]:
+        remote(crecv.at[n], crecv.at[n], t_send.at[n], t_recv.at[n], (g, sibling)).wait_recv()
     total = crecv[0]
-    for s in range(1, nd):
-        total = total + crecv[s]
-    o_comp[...] = (total[:, 0:pb] / jnp.maximum(total[:, pb : pb + 1], 1.0)).astype(jnp.bfloat16)
+    for n in range(1, nz):
+        total = total + crecv[n]
+    o_comp[...] = (total / jnp.maximum(number[:, 0:1], 1.0)).astype(jnp.bfloat16)
 
     for copy in sent:
         copy.wait_send()
     for it in range(ITERS):
-        for r in range(regimes):
-            @pl.when(d != r)
+        for n in range(pairs_of):
+            r = 2 * n + core
+            remote(msend.at[it, r], msib.at[it, n], s_send.at[it, n], s_recv.at[it, n], (g, sibling)).wait_send()
+
+            @pl.when(z != n)
             def _():
-                remote(msend.at[it, r], msend.at[it, r], m_send.at[it, r], m_recv.at[it, 0], (g, r)).wait_send()
+                remote(chip.at[it, n], mrecv.at[it, z], m_send.at[it, n], m_recv.at[it, z], (g, r)).wait_send()
+                remote(res.at[it, r], res.at[it, r], r_fwd.at[it, n], r_recv.at[it, r], (g, sibling)).wait_send()
+                if it == ITERS - 1:
+                    remote(cres.at[r], cres.at[r], c_fwd.at[n], c_recv.at[r], (g, sibling)).wait_send()
 
         def own_sent():
             for k in range(1, ng):
                 remote(gslot.at[it, g], gslot.at[it, g], g_send.at[it, k - 1], g_recv.at[it, 0], (grid_peer(k), d)).wait_send()
-            for k in range(1, nd):
-                remote(res.at[it, d], res.at[it, d], r_send.at[it, k - 1], r_recv.at[it, 0], (g, day_peer(k))).wait_send()
+            for n, target in enumerate(near):
+                remote(res.at[it, d], res.at[it, d], r_send.at[it, n], r_recv.at[it, d], (g, target)).wait_send()
                 if it == ITERS - 1:
-                    remote(cres.at[d], cres.at[d], c_send.at[k - 1], c_recv.at[0], (g, day_peer(k))).wait_send()
+                    remote(cres.at[d], cres.at[d], c_send.at[n], c_recv.at[d], (g, target)).wait_send()
 
         if nd > regimes:
             pl.when(d < regimes)(own_sent)
         else:
             own_sent()
+
+
+def hand_over(*refs):
+    n = (len(refs) - 1) // 2
+    copies = [pltpu.make_async_copy(refs[i], refs[n + i], refs[-1].at[i]) for i in range(n)]
+    for copy in copies:
+        copy.start()
+    for copy in copies:
+        copy.wait()
 
 
 def solution(mesh):
@@ -361,6 +419,7 @@
         regimes = means_init.shape[0]
         dl = days // ng
         half = width // 2
+        nz = nd // 2
         f32 = jnp.float32
         vmem = pl.BlockSpec(memory_space=pltpu.VMEM)
         dma = pltpu.SemaphoreType.DMA
@@ -384,39 +443,61 @@
                 pltpu.VMEM((ng, width, dl), f32),
                 pltpu.VMEM((ng, width, dl), f32),
                 pltpu.VMEM((ITERS, regimes, half + 8, 2 * width), f32),
-                pltpu.VMEM((ITERS, nd, half + 8, 2 * width), f32),
+                pltpu.VMEM((ITERS, regimes // 2, half + 8, 2 * width), f32),
+                pltpu.VMEM((ITERS, regimes // 2, half + 8, 2 * width), f32),
+                pltpu.VMEM((ITERS, nz, half + 8, 2 * width), f32),
                 pltpu.VMEM((ITERS, ng, half + 8, 2 * width), f32),
                 pltpu.VMEM((ITERS, regimes, half + 8, 2 * width), f32),
                 pltpu.VMEM((regimes, half, 2 * width), f32),
                 pltpu.VMEM((ng, regimes, dl), f32),
-                pltpu.VMEM((nd - 1, regimes, pb + 128), f32),
-                pltpu.VMEM((nd, regimes, pb + 128), f32),
+                pltpu.VMEM((nz, regimes, pb), f32),
+                pltpu.VMEM((nz, regimes, pb), f32),
+                pltpu.VMEM((nz, regimes, pb), f32),
+                pltpu.VMEM((nz, regimes, pb), f32),
+                pltpu.VMEM((nd, regimes, 128), f32),
                 dma((nd,)),
-                dma((nd // 2,)),
-                dma((nd // 2,)),
+                dma((nz,)),
+                dma((nz,)),
                 dma((nd,)),
                 dma((ng,)),
                 dma((ng,)),
-                dma((ITERS, regimes)),
-                dma((ITERS, nd)),
+                dma((ITERS, regimes // 2)),
+                dma((ITERS, regimes // 2)),
+                dma((ITERS, regimes // 2)),
+                dma((ITERS, nz)),
                 dma((ITERS, ng)),
                 dma((ITERS, ng)),
-                dma((ITERS, nd)),
+                dma((ITERS, nz)),
+                dma((ITERS, regimes // 2)),
                 dma((ITERS, regimes)),
-                dma((nd,)),
+                dma((nz,)),
+                dma((regimes // 2,)),
                 dma((regimes,)),
                 dma((ng,)),
                 dma((ng,)),
+                dma((nz,)),
+                dma((nz,)),
+                dma((nz,)),
+                dma((nz,)),
                 dma((nd,)),
                 dma((nd,)),
                 dma((4,)),
             ],
             compiler_params=pltpu.CompilerParams(
-                collective_id=0, has_side_effects=True, vmem_limit_bytes=48 * 1024 * 1024
+                collective_id=0, has_side_effects=True, vmem_limit_bytes=60 * 1024 * 1024
             ),
             name="regimes",
         )(anomalies, eofs, means_init, variances, mixing)
-        return outs
+        anywhere = pl.BlockSpec(memory_space=pltpu.HBM)
+        return pl.pallas_call(
+            hand_over,
+            out_shape=tuple(jax.ShapeDtypeStruct(o.shape, o.dtype) for o in outs),
+            in_specs=[anywhere] * len(outs),
+            out_specs=(anywhere,) * len(outs),
+            scratch_shapes=[dma((len(outs),))],
+            compiler_params=pltpu.CompilerParams(vmem_limit_bytes=60 * 1024 * 1024),
+            name="hand_over",
+        )(*outs)
 
     in_specs = (P("day", "grid"), P(None, ("grid", "day")), P(), P(), P())
     out_specs = (P(), P(), P(), P(None, "day"), P(None, ("grid", "day")))

time: 71.6 us -> 76.3 us (1.066)
  Pallas kernels: 64.9 us -> 75.5 us
  local copies, waits for them, and re-layouts: 5.88 us -> 0 us
    pallas_call x0 -> x1, Pallas kernels: none -> 10.5 us  [body(): pl.pallas_call(hand_over, out_shape=tuple((jax.ShapeDtypeStruct(o.shape,...]
    unnamed x13 -> x0, local copies, waits for them, and re-layouts: 5.88 us -> none
where the time goes in v3:
time: 76.3 us; the launch traced here: 76.1 us
  Pallas kernels  75.5 us (99%)
    pallas_call x1, Pallas kernels, body(): pl.pallas_call(functools.partial(kernel, ng, nd, regimes, width, dl, pb),...  65 us
    pallas_call x1, Pallas kernels, body(): pl.pallas_call(hand_over, out_shape=tuple((jax.ShapeDtypeStruct(o.shape,...  10.5 us

profile of v3, /device:TPU:0, one launch (start us, length us, event | category | flops | bytes accessed | tf_op | source)
XLA Modules:
  0.0 76.1 jit_solution(17801738961006480386)
XLA Ops:
  0.6 65.0 %regimes.1 = (f32[8,64]{1,0:T(8,128)}, f32[8,64,64]{2,1,0:T(8,128)}, f32[8]{0:T(128)}, f32[8,1024]{1,0:T(8,128)}, bf16[8,512]{1,0:T(8,128)(2,1)}) custom-call(bf16[1024,4096]{1,0:T(8,128)(2,1)} %anom_hbm.1, bf16[64,512]{1,0:T(8,128)(2,1)} %eofs_ref.1, f32[8,64]{1,0:T(8,128)} %means_hbm.1, f32[8,64]{1,0:T(8,128)} %var_hbm.1, f32[8]{0:T(128)} %mix_hbm.1), custom_call_target="tpu_custom_call" | custom-call | tf_op jit(solution)/shard_map/regimes/pallas_call | solution.py:426
  65.6 10.5 %hand_over.1 = (f32[8,64]{1,0:T(8,128)}, f32[8,64,64]{2,1,0:T(8,128)}, f32[8]{0:T(128)}, f32[8,1024]{1,0:T(8,128)}, bf16[8,512]{1,0:T(8,128)(2,1)}) custom-call(f32[8,64]{1,0:T(8,128)} %get-tuple-element.10.refs_0_, f32[8,64,64]{2,1,0:T(8,128)} %get-tuple-element.11.refs_1_, f32[8]{0:T(128)} %get-tuple-element.12.refs_2_, ...), custom_call_target="tpu_custom_call" | custom-call | tf_op jit(solution)/shard_map/hand_over/pallas_call | solution.py:492

commit v4 on v3

--- a/solution.py
+++ b/solution.py
@@ -63,7 +63,7 @@
     ng, nd, regimes, width, dl, pb,
     anom_hbm, eofs_ref, means_hbm, var_hbm, mix_hbm,
     o_means, o_covs, o_weights, o_member, o_comp,
-    means_ref, var_ref, mix_ref, anom, eall, acc, pin, msend, msib, chip, mrecv, gslot, res, cres, memall, cout, cin, csend, crecv, cnt,
+    means_ref, var_ref, mix_ref, anom, eall, acc, pout, pin, msend, msib, chip, mrecv, gslot, res, cres, memall, cacc, cout, cin, csend, crecv, cnt,
     anom_sem, e_send, e_fwd, e_recv, p_send, p_recv, s_send, s_recv, m_send, m_recv, g_send, g_recv,
     r_send, r_fwd, r_recv, c_send, c_fwd, c_recv, y_send, y_recv, u_send, u_recv, t_send, t_recv, n_send, n_recv, i_sem,
 ):
@@ -133,9 +133,8 @@
         copy.start()
         sent.append(copy)
 
-    def project(s, block, i):
-        days = anom[s, pl.ds(pl.multiple_of(i * dl, dl), dl), :]
-        return lax.dot_general(block, days, NT, preferred_element_type=jnp.float32)
+    def part(i):
+        return pl.ds(pl.multiple_of(i * dl, dl), dl)
 
     count = 0
     for n, pair in enumerate(pairs):
@@ -153,32 +152,23 @@
             load(s).wait()
             count += 1
             if count < nd:
-                first = count == 1
-
-                def add(i, carry):
-                    term = project(s, block, i)
-                    acc[i] = term if first else acc[i] + term
-                    return carry
-
-                if ng <= 4:
-                    for i in range(ng):
-                        add(i, 0)
-                else:
-                    lax.fori_loop(0, ng, add, 0)
+                term = lax.dot_general(anom[s], block, NT, preferred_element_type=jnp.float32)
+                acc[...] = term if count == 1 else acc[...] + term
             else:
                 for k in list(range(1, ng)) + [0]:
                     i = grid_peer(k)
-                    total = acc[i] + project(s, block, i)
+                    term = lax.dot_general(anom[s, part(i), :], block, NT, preferred_element_type=jnp.float32)
+                    total = (acc[part(i), :] + term).T
                     if k == 0:
                         pin[g] = total
                     else:
-                        acc[i] = total
-                        copy = remote(acc.at[i], pin.at[g], p_send.at[k - 1], p_recv.at[g], (i, d))
+                        pout[i] = total
+                        copy = remote(pout.at[i], pin.at[g], p_send.at[k - 1], p_recv.at[g], (i, d))
                         copy.start()
                         sent.append(copy)
     for k in range(1, ng):
         i = grid_peer(k)
-        remote(acc.at[i], pin.at[i], p_send.at[k - 1], p_recv.at[i], (i, d)).wait_recv()
+        remote(pout.at[i], pin.at[i], p_send.at[k - 1], p_recv.at[i], (i, d)).wait_recv()
     x = pin[0]
     for i in range(1, ng):
         x = x + pin[i]
@@ -310,6 +300,9 @@
         copy = remote(memall.at[g], memall.at[g], y_send.at[k - 1], y_recv.at[g], (grid_peer(k), d))
         copy.start()
         sent.append(copy)
+    mine = resp.astype(jnp.bfloat16)
+    for s in range(nd):
+        cacc[s] = jnp.dot(mine, anom[s, part(g), :], preferred_element_type=jnp.float32)
     o_means[...] = means
     o_weights[...] = jnp.sum(jnp.where(er == ec, weights, 0.0), axis=0)
     for k in range(1, ng):
@@ -322,11 +315,23 @@
         copy = remote(cnt.at[d], cnt.at[d], n_send.at[k - 1], n_recv.at[d], (g, day_peer(k)))
         copy.start()
         sent.append(copy)
-    rounded = member.astype(jnp.bfloat16)
+
+    def field_sums(s):
+        def add(k, total):
+            i = grid_peer(k)
+            days = memall[i].astype(jnp.bfloat16)
+            return total + jnp.dot(days, anom[s, part(i), :], preferred_element_type=jnp.float32)
+
+        total = cacc[s]
+        if ng > 4:
+            return lax.fori_loop(1, ng, add, total)
+        for k in range(1, ng):
+            total = add(k, total)
+        return total
 
     order = [lax.rem(z + o, nz) for o in reversed(offsets)] + [z]
     for n in order:
-        cout[n] = jnp.dot(rounded, anom[2 * n + 1 - core], preferred_element_type=jnp.float32)
+        cout[n] = field_sums(2 * n + 1 - core)
         copy = remote(cout.at[n], cin.at[n], u_send.at[n], u_recv.at[n], (g, sibling))
         copy.start()
         sent.append(copy)
@@ -341,7 +346,7 @@
             copy.start()
 
     for n in order:
-        terms = jnp.dot(rounded, anom[2 * n + core], preferred_element_type=jnp.float32)
+        terms = field_sums(2 * n + core)
         remote(cin.at[n], cin.at[n], u_send.at[n], u_recv.at[n], (g, sibling)).wait_recv()
         terms = terms + cin[n]
         if n is z:
@@ -402,12 +407,9 @@
 
 
 def hand_over(*refs):
-    n = (len(refs) - 1) // 2
-    copies = [pltpu.make_async_copy(refs[i], refs[n + i], refs[-1].at[i]) for i in range(n)]
-    for copy in copies:
-        copy.start()
-    for copy in copies:
-        copy.wait()
+    n = len(refs) // 2
+    for i in range(n):
+        refs[n + i][...] = refs[i][...]
 
 
 def solution(mesh):
@@ -440,6 +442,7 @@
                 pltpu.VMEM((regimes,), f32),
                 pltpu.VMEM((nd, days, pb), jnp.bfloat16),
                 pltpu.VMEM((nd, width, pb), jnp.bfloat16),
+                pltpu.VMEM((days, width), f32),
                 pltpu.VMEM((ng, width, dl), f32),
                 pltpu.VMEM((ng, width, dl), f32),
                 pltpu.VMEM((ITERS, regimes, half + 8, 2 * width), f32),
@@ -450,6 +453,7 @@
                 pltpu.VMEM((ITERS, regimes, half + 8, 2 * width), f32),
                 pltpu.VMEM((regimes, half, 2 * width), f32),
                 pltpu.VMEM((ng, regimes, dl), f32),
+                pltpu.VMEM((nd, regimes, pb), f32),
                 pltpu.VMEM((nz, regimes, pb), f32),
                 pltpu.VMEM((nz, regimes, pb), f32),
                 pltpu.VMEM((nz, regimes, pb), f32),
@@ -488,13 +492,11 @@
             ),
             name="regimes",
         )(anomalies, eofs, means_init, variances, mixing)
-        anywhere = pl.BlockSpec(memory_space=pltpu.HBM)
         return pl.pallas_call(
             hand_over,
             out_shape=tuple(jax.ShapeDtypeStruct(o.shape, o.dtype) for o in outs),
-            in_specs=[anywhere] * len(outs),
-            out_specs=(anywhere,) * len(outs),
-            scratch_shapes=[dma((len(outs),))],
+            in_specs=[vmem] * len(outs),
+            out_specs=(vmem,) * len(outs),
             compiler_params=pltpu.CompilerParams(vmem_limit_bytes=60 * 1024 * 1024),
             name="hand_over",
         )(*outs)

time: 76.3 us -> 67.2 us (0.88)
  Pallas kernels: 75.5 us -> 66.4 us
    pallas_call x1, Pallas kernels: 10.5 us -> 1.68 us  [body(): pl.pallas_call(hand_over, out_shape=tuple((jax.ShapeDtypeStruct(o.shape,...]
where the time goes in v4:
time: 67.2 us; the launch traced here: 67 us
  Pallas kernels  66.4 us (99%)
    pallas_call x1, Pallas kernels, body(): pl.pallas_call(functools.partial(kernel, ng, nd, regimes, width, dl, pb),...  64.7 us
    pallas_call x1, Pallas kernels, body(): pl.pallas_call(hand_over, out_shape=tuple((jax.ShapeDtypeStruct(o.shape,...  1.68 us

profile of v4, /device:TPU:0, one launch (start us, length us, event | category | flops | bytes accessed | tf_op | source)
XLA Modules:
  0.0 67.0 jit_solution(6989608057187082085)
XLA Ops:
  0.6 64.7 %regimes.1 = (f32[8,64]{1,0:T(8,128)}, f32[8,64,64]{2,1,0:T(8,128)}, f32[8]{0:T(128)}, f32[8,1024]{1,0:T(8,128)}, bf16[8,512]{1,0:T(8,128)(2,1)}) custom-call(bf16[1024,4096]{1,0:T(8,128)(2,1)} %anom_hbm.1, bf16[64,512]{1,0:T(8,128)(2,1)} %eofs_ref.1, f32[8,64]{1,0:T(8,128)} %means_hbm.1, f32[8,64]{1,0:T(8,128)} %var_hbm.1, f32[8]{0:T(128)} %mix_hbm.1), custom_call_target="tpu_custom_call" | custom-call | tf_op jit(solution)/shard_map/regimes/pallas_call | solution.py:428
  65.3 1.7 %hand_over.1 = (f32[8,64]{1,0:T(8,128)}, f32[8,64,64]{2,1,0:T(8,128)}, f32[8]{0:T(128)}, f32[8,1024]{1,0:T(8,128)}, bf16[8,512]{1,0:T(8,128)(2,1)}) custom-call(f32[8,64]{1,0:T(8,128)} %get-tuple-element.10.refs_0_, f32[8,64,64]{2,1,0:T(8,128)} %get-tuple-element.11.refs_1_, f32[8]{0:T(128)} %get-tuple-element.12.refs_2_, ...), custom_call_target="tpu_custom_call" | custom-call | tf_op jit(solution)/shard_map/hand_over/pallas_call | solution.py:495

commit v5 on v4

--- a/solution.py
+++ b/solution.py
@@ -42,18 +42,22 @@
             [jnp.broadcast_to(rows[bb][:, 8 * b + k : 8 * b + k + 1], wide) for bb in range(b, blocks)]
             for k in range(8)
         ]
-        for s in range(8):
-            inverse = 1.0 / jnp.broadcast_to(cols[s][0][s : s + 1, :], wide)
-            pivot_row = jnp.broadcast_to(rows[b][s : s + 1, :], wide)
-            later = [jnp.broadcast_to(cols[k][0][s : s + 1, :], wide) for k in range(s + 1, 8)]
+        for s in range(0, 8, 2):
+            spread = [[jnp.broadcast_to(v[t : t + 1, :], wide) for t in (s, s + 1)] for v in [rows[b]] + [c[0] for c in cols]]
+            (top, mid), low = spread[1 + s], spread[2 + s][1]
+            inverse = 1.0 / (top * low - mid * mid)
             for n in range(blocks - b):
-                column = cols[s][n]
+                one, two = cols[s][n], cols[s + 1][n]
+                f = (one * low - two * mid) * inverse
+                h = (two * top - one * mid) * inverse
+                row_f = f
                 if n == 0:
-                    column = jnp.where(sub > s, column, 0.0)
-                factor = column * inverse
-                for k in range(s + 1, 8):
-                    cols[k][n] = cols[k][n] - factor * later[k - s - 1]
-                rows[b + n] = rows[b + n] - factor * pivot_row
+                    f = jnp.where(sub > s + 1, f, 0.0)
+                    h = jnp.where(sub > s + 1, h, 0.0)
+                    row_f = jnp.where(sub == s + 1, mid / top, f)
+                for k in range(s + 2, 8):
+                    cols[k][n] = cols[k][n] - (f * spread[1 + k][0] + h * spread[1 + k][1])
+                rows[b + n] = rows[b + n] - (row_f * spread[0][0] + h * spread[0][1])
     full = jnp.concatenate(rows, axis=0)
     diag = jnp.sum(full[:, :width] * eye, axis=1, keepdims=True)
     return full * lax.rsqrt(diag), diag
@@ -63,7 +67,7 @@
     ng, nd, regimes, width, dl, pb,
     anom_hbm, eofs_ref, means_hbm, var_hbm, mix_hbm,
     o_means, o_covs, o_weights, o_member, o_comp,
-    means_ref, var_ref, mix_ref, anom, eall, acc, pout, pin, msend, msib, chip, mrecv, gslot, res, cres, memall, cacc, cout, cin, csend, crecv, cnt,
+    means_ref, var_ref, mix_ref, anom, eall, acc, pout, pin, dbuf, rbuf, qbuf, msend, msib, chip, mrecv, gslot, res, cres, memall, cacc, cout, cin, csend, crecv, cnt,
     anom_sem, e_send, e_fwd, e_recv, p_send, p_recv, s_send, s_recv, m_send, m_recv, g_send, g_recv,
     r_send, r_fwd, r_recv, c_send, c_fwd, c_recv, y_send, y_recv, u_send, u_recv, t_send, t_recv, n_send, n_recv, i_sem,
 ):
@@ -108,6 +112,9 @@
     ]
     for copy in first_copies:
         copy.start()
+    places = list(range(pairs_of))
+    if pairs_of == nz:
+        places = [lax.rem(z + o, nz) for o in reversed(offsets)] + [z]
     pairs = block_pairs()
     for pair in pairs:
         for s in pair:
@@ -186,7 +193,8 @@
     logdet = 0.5 * jnp.sum(jnp.log(variances), axis=1, keepdims=True)
     quad = []
     for r in range(regimes):
-        y = (x - mcol[:, r : r + 1]) * scale[:, r : r + 1]
+        dbuf[r] = x - mcol[:, r : r + 1]
+        y = dbuf[r] * scale[:, r : r + 1]
         quad.append(jnp.sum(y * y, axis=0, keepdims=True))
     resp = softmax_regimes(logw - logdet - 0.5 * jnp.concatenate(quad, axis=0))
 
@@ -196,28 +204,29 @@
     eye = (ei == ej).astype(jnp.float32)
 
     for it in range(ITERS):
-        counts = jnp.sum(resp, axis=1, keepdims=True)
-        for r in range(regimes):
-            diff = x - mcol[:, r : r + 1]
-            lhs = jnp.concatenate([diff * resp[r : r + 1, :], resp], axis=0)
+        rbuf[...] = resp
+
+        def moments(r):
+            diff = dbuf[r]
+            share = rbuf[pl.ds(r, 1), :]
+            lhs = jnp.concatenate([diff * share, jnp.broadcast_to(share, (8, dl))], axis=0)
             out = lax.dot_general(lhs, diff, NT, precision=PRECISE, preferred_element_type=jnp.float32)
-            msend[it, r, 0:half, :] = jnp.concatenate([out[0:half], out[half:width]], axis=1)
-            first = jnp.broadcast_to(out[width + r : width + r + 1, :], (8, width))
-            number = jnp.broadcast_to(counts[r : r + 1, :], (8, width))
-            msend[it, r, half : half + 8, :] = jnp.concatenate([first, number], axis=1)
-
-            @pl.when(core != r % 2)
-            def _():
-                remote(msend.at[it, r], msib.at[it, r // 2], s_send.at[it, r // 2], s_recv.at[it, r // 2], (g, sibling)).start()
-
-        for n in range(pairs_of):
-            mine = 2 * n + core
+            number = jnp.broadcast_to(jnp.sum(share, axis=1, keepdims=True), (8, width))
+            second = jnp.concatenate([out[0:half], out[half:width]], axis=1)
+            return second, jnp.concatenate([out[width : width + 8], number], axis=1)
+
+        for n in places:
+            msend[it, n, 0:half, :], msend[it, n, half : half + 8, :] = moments(2 * n + 1 - core)
+            remote(msend.at[it, n], msib.at[it, n], s_send.at[it, n], s_recv.at[it, n], (g, sibling)).start()
+        for n in places:
+            second, tail = moments(2 * n + core)
             remote(msib.at[it, n], msib.at[it, n], s_send.at[it, n], s_recv.at[it, n], (g, sibling)).wait_recv()
-            chip[it, n] = msend[it, mine] + msib[it, n]
+            chip[it, n, 0:half, :] = second + msib[it, n, 0:half, :]
+            chip[it, n, half : half + 8, :] = tail + msib[it, n, half : half + 8, :]
 
             @pl.when(z != n)
             def _():
-                remote(chip.at[it, n], mrecv.at[it, z], m_send.at[it, n], m_recv.at[it, z], (g, mine)).start()
+                remote(chip.at[it, n], mrecv.at[it, z], m_send.at[it, n], m_recv.at[it, z], (g, 2 * n + core)).start()
 
         def own():
             mrecv[it, z] = chip[it, z]
@@ -268,7 +277,16 @@
         else:
             own()
 
-        for n in range(pairs_of):
+        def distance(r):
+            mean = columns_of(res[it, r, half : half + 8, 0:width])[:, 0:1]
+            folded = res[it, r, 0:half, :]
+            factor = jnp.concatenate([folded[:, 0:width], folded[:, width : 2 * width]], axis=0)
+            diff = x - mean
+            dbuf[r] = diff
+            y = jnp.dot(factor, diff, precision=PRECISE, preferred_element_type=jnp.float32)
+            qbuf[pl.ds(r, 1), :] = jnp.sum(y * y, axis=0, keepdims=True)
+
+        for n in reversed(places):
             r = 2 * n + core
 
             @pl.when(z != n)
@@ -277,22 +295,17 @@
                 copy.wait_recv()
                 copy.start()
 
-        for n in range(pairs_of):
+            distance(r)
+        for n in reversed(places):
             r = 2 * n + 1 - core
             remote(res.at[it, r], res.at[it, r], r_fwd.at[it, n], r_recv.at[it, r], (g, sibling)).wait_recv()
+            distance(r)
 
         means = jnp.concatenate([res[it, r, half : half + 1, 0:width] for r in range(regimes)], axis=0)
         tails = jnp.concatenate([res[it, r, half : half + 1, width : 2 * width] for r in range(regimes)], axis=0)
         counted = tails[:, 0:1]
         weights = counted / jnp.sum(counted, axis=0, keepdims=True)
-        mcol = columns_of(means)
-        quad = []
-        for r in range(regimes):
-            folded = res[it, r, 0:half, :]
-            factor = jnp.concatenate([folded[:, 0:width], folded[:, width : 2 * width]], axis=0)
-            y = jnp.dot(factor, x - mcol[:, r : r + 1], precision=PRECISE, preferred_element_type=jnp.float32)
-            quad.append(jnp.sum(y * y, axis=0, keepdims=True))
-        logp = jnp.log(weights) - tails[:, half : half + 1] - 0.5 * jnp.concatenate(quad, axis=0)
+        logp = jnp.log(weights) - tails[:, half : half + 1] - 0.5 * qbuf[...]
         resp = softmax_regimes(logp)
 
     memall[g] = resp
@@ -383,7 +396,7 @@
     for it in range(ITERS):
         for n in range(pairs_of):
             r = 2 * n + core
-            remote(msend.at[it, r], msib.at[it, n], s_send.at[it, n], s_recv.at[it, n], (g, sibling)).wait_send()
+            remote(msend.at[it, n], msib.at[it, n], s_send.at[it, n], s_recv.at[it, n], (g, sibling)).wait_send()
 
             @pl.when(z != n)
             def _():
@@ -445,7 +458,10 @@
                 pltpu.VMEM((days, width), f32),
                 pltpu.VMEM((ng, width, dl), f32),
                 pltpu.VMEM((ng, width, dl), f32),
-                pltpu.VMEM((ITERS, regimes, half + 8, 2 * width), f32),
+                pltpu.VMEM((regimes, width, dl), f32),
+                pltpu.VMEM((regimes, dl), f32),
+                pltpu.VMEM((regimes, dl), f32),
+                pltpu.VMEM((ITERS, regimes // 2, half + 8, 2 * width), f32),
                 pltpu.VMEM((ITERS, regimes // 2, half + 8, 2 * width), f32),
                 pltpu.VMEM((ITERS, regimes // 2, half + 8, 2 * width), f32),
                 pltpu.VMEM((ITERS, nz, half + 8, 2 * width), f32),

time: 67.2 us -> 72.6 us (1.080)
  Pallas kernels: 66.4 us -> 71.8 us
    pallas_call x1, Pallas kernels: 64.7 us -> 70.1 us  [body(): pl.pallas_call(functools.partial(kernel, ng, nd, regimes, width, dl, pb),...]
where the time goes in v5:
time: 72.6 us; the launch traced here: 72.4 us
  Pallas kernels  71.8 us (99%)
    pallas_call x1, Pallas kernels, body(): pl.pallas_call(functools.partial(kernel, ng, nd, regimes, width, dl, pb),...  70.1 us
    pallas_call x1, Pallas kernels, body(): pl.pallas_call(hand_over, out_shape=tuple((jax.ShapeDtypeStruct(o.shape,...  1.68 us

profile of v5, /device:TPU:0, one launch (start us, length us, event | category | flops | bytes accessed | tf_op | source)
XLA Modules:
  0.0 72.4 jit_solution(3601372632808528999)
XLA Ops:
  0.6 70.1 %regimes.1 = (f32[8,64]{1,0:T(8,128)}, f32[8,64,64]{2,1,0:T(8,128)}, f32[8]{0:T(128)}, f32[8,1024]{1,0:T(8,128)}, bf16[8,512]{1,0:T(8,128)(2,1)}) custom-call(bf16[1024,4096]{1,0:T(8,128)(2,1)} %anom_hbm.1, bf16[64,512]{1,0:T(8,128)(2,1)} %eofs_ref.1, f32[8,64]{1,0:T(8,128)} %means_hbm.1, f32[8,64]{1,0:T(8,128)} %var_hbm.1, f32[8]{0:T(128)} %mix_hbm.1), custom_call_target="tpu_custom_call" | custom-call | tf_op jit(solution)/shard_map/regimes/pallas_call | solution.py:441
  70.8 1.7 %hand_over.1 = (f32[8,64]{1,0:T(8,128)}, f32[8,64,64]{2,1,0:T(8,128)}, f32[8]{0:T(128)}, f32[8,1024]{1,0:T(8,128)}, bf16[8,512]{1,0:T(8,128)(2,1)}) custom-call(f32[8,64]{1,0:T(8,128)} %get-tuple-element.10.refs_0_, f32[8,64,64]{2,1,0:T(8,128)} %get-tuple-element.11.refs_1_, f32[8]{0:T(128)} %get-tuple-element.12.refs_2_, ...), custom_call_target="tpu_custom_call" | custom-call | tf_op jit(solution)/shard_map/hand_over/pallas_call | solution.py:511

commit v6 on v5

--- a/solution.py
+++ b/solution.py
@@ -217,12 +217,13 @@
 
         for n in places:
             msend[it, n, 0:half, :], msend[it, n, half : half + 8, :] = moments(2 * n + 1 - core)
+        for n in places:
             remote(msend.at[it, n], msib.at[it, n], s_send.at[it, n], s_recv.at[it, n], (g, sibling)).start()
         for n in places:
-            second, tail = moments(2 * n + core)
+            chip[it, n, 0:half, :], chip[it, n, half : half + 8, :] = moments(2 * n + core)
+        for n in places:
             remote(msib.at[it, n], msib.at[it, n], s_send.at[it, n], s_recv.at[it, n], (g, sibling)).wait_recv()
-            chip[it, n, 0:half, :] = second + msib[it, n, 0:half, :]
-            chip[it, n, half : half + 8, :] = tail + msib[it, n, half : half + 8, :]
+            chip[it, n] = chip[it, n] + msib[it, n]
 
             @pl.when(z != n)
             def _():
@@ -277,14 +278,16 @@
         else:
             own()
 
-        def distance(r):
-            mean = columns_of(res[it, r, half : half + 8, 0:width])[:, 0:1]
-            folded = res[it, r, 0:half, :]
-            factor = jnp.concatenate([folded[:, 0:width], folded[:, width : 2 * width]], axis=0)
-            diff = x - mean
-            dbuf[r] = diff
-            y = jnp.dot(factor, diff, precision=PRECISE, preferred_element_type=jnp.float32)
-            qbuf[pl.ds(r, 1), :] = jnp.sum(y * y, axis=0, keepdims=True)
+        def distances(batch):
+            centres = [res[it, r, half : half + 1, 0:width] for r in batch]
+            centres = columns_of(jnp.concatenate(centres + centres[: -len(batch) % 8], axis=0))
+            for n, r in enumerate(batch):
+                folded = res[it, r, 0:half, :]
+                factor = jnp.concatenate([folded[:, 0:width], folded[:, width : 2 * width]], axis=0)
+                diff = x - centres[:, n : n + 1]
+                dbuf[r] = diff
+                y = jnp.dot(factor, diff, precision=PRECISE, preferred_element_type=jnp.float32)
+                qbuf[pl.ds(r, 1), :] = jnp.sum(y * y, axis=0, keepdims=True)
 
         for n in reversed(places):
             r = 2 * n + core
@@ -295,11 +298,11 @@
                 copy.wait_recv()
                 copy.start()
 
-            distance(r)
+        distances([2 * n + core for n in reversed(places)])
         for n in reversed(places):
             r = 2 * n + 1 - core
             remote(res.at[it, r], res.at[it, r], r_fwd.at[it, n], r_recv.at[it, r], (g, sibling)).wait_recv()
-            distance(r)
+        distances([2 * n + 1 - core for n in reversed(places)])
 
         means = jnp.concatenate([res[it, r, half : half + 1, 0:width] for r in range(regimes)], axis=0)
         tails = jnp.concatenate([res[it, r, half : half + 1, width : 2 * width] for r in range(regimes)], axis=0)

time: 72.6 us -> 68.5 us (0.944)
  Pallas kernels: 71.8 us -> 67.7 us
    pallas_call x1, Pallas kernels: 70.1 us -> 66 us  [body(): pl.pallas_call(functools.partial(kernel, ng, nd, regimes, width, dl, pb),...]
where the time goes in v6:
time: 68.5 us; the launch traced here: 68.3 us
  Pallas kernels  67.7 us (99%)
    pallas_call x1, Pallas kernels, body(): pl.pallas_call(functools.partial(kernel, ng, nd, regimes, width, dl, pb),...  66 us
    pallas_call x1, Pallas kernels, body(): pl.pallas_call(hand_over, out_shape=tuple((jax.ShapeDtypeStruct(o.shape,...  1.68 us

profile of v6, /device:TPU:0, one launch (start us, length us, event | category | flops | bytes accessed | tf_op | source)
XLA Modules:
  0.0 68.3 jit_solution(15630468737021245576)
XLA Ops:
  0.6 66.0 %regimes.1 = (f32[8,64]{1,0:T(8,128)}, f32[8,64,64]{2,1,0:T(8,128)}, f32[8]{0:T(128)}, f32[8,1024]{1,0:T(8,128)}, bf16[8,512]{1,0:T(8,128)(2,1)}) custom-call(bf16[1024,4096]{1,0:T(8,128)(2,1)} %anom_hbm.1, bf16[64,512]{1,0:T(8,128)(2,1)} %eofs_ref.1, f32[8,64]{1,0:T(8,128)} %means_hbm.1, f32[8,64]{1,0:T(8,128)} %var_hbm.1, f32[8]{0:T(128)} %mix_hbm.1), custom_call_target="tpu_custom_call" | custom-call | tf_op jit(solution)/shard_map/regimes/pallas_call | solution.py:444
  66.6 1.7 %hand_over.1 = (f32[8,64]{1,0:T(8,128)}, f32[8,64,64]{2,1,0:T(8,128)}, f32[8]{0:T(128)}, f32[8,1024]{1,0:T(8,128)}, bf16[8,512]{1,0:T(8,128)(2,1)}) custom-call(f32[8,64]{1,0:T(8,128)} %get-tuple-element.10.refs_0_, f32[8,64,64]{2,1,0:T(8,128)} %get-tuple-element.11.refs_1_, f32[8]{0:T(128)} %get-tuple-element.12.refs_2_, ...), custom_call_target="tpu_custom_call" | custom-call | tf_op jit(solution)/shard_map/hand_over/pallas_call | solution.py:514

commit v7 on v4

--- a/solution.py
+++ b/solution.py
@@ -206,6 +206,7 @@
             number = jnp.broadcast_to(counts[r : r + 1, :], (8, width))
             msend[it, r, half : half + 8, :] = jnp.concatenate([first, number], axis=1)
 
+        for r in range(regimes):
             @pl.when(core != r % 2)
             def _():
                 remote(msend.at[it, r], msib.at[it, r // 2], s_send.at[it, r // 2], s_recv.at[it, r // 2], (g, sibling)).start()

time: 67.2 us -> 67.9 us (1.010)
  Pallas kernels: 66.4 us -> 67.1 us
    pallas_call x1, Pallas kernels: 64.7 us -> 65.4 us  [body(): pl.pallas_call(functools.partial(kernel, ng, nd, regimes, width, dl, pb),...]
where the time goes in v7:
time: 67.9 us; the launch traced here: 67.7 us
  Pallas kernels  67.1 us (99%)
    pallas_call x1, Pallas kernels, body(): pl.pallas_call(functools.partial(kernel, ng, nd, regimes, width, dl, pb),...  65.4 us
    pallas_call x1, Pallas kernels, body(): pl.pallas_call(hand_over, out_shape=tuple((jax.ShapeDtypeStruct(o.shape,...  1.68 us

profile of v7, /device:TPU:0, one launch (start us, length us, event | category | flops | bytes accessed | tf_op | source)
XLA Modules:
  0.0 67.7 jit_solution(15416803893590422148)
XLA Ops:
  0.6 65.4 %regimes.1 = (f32[8,64]{1,0:T(8,128)}, f32[8,64,64]{2,1,0:T(8,128)}, f32[8]{0:T(128)}, f32[8,1024]{1,0:T(8,128)}, bf16[8,512]{1,0:T(8,128)(2,1)}) custom-call(bf16[1024,4096]{1,0:T(8,128)(2,1)} %anom_hbm.1, bf16[64,512]{1,0:T(8,128)(2,1)} %eofs_ref.1, f32[8,64]{1,0:T(8,128)} %means_hbm.1, f32[8,64]{1,0:T(8,128)} %var_hbm.1, f32[8]{0:T(128)} %mix_hbm.1), custom_call_target="tpu_custom_call" | custom-call | tf_op jit(solution)/shard_map/regimes/pallas_call | solution.py:429
  66.0 1.7 %hand_over.1 = (f32[8,64]{1,0:T(8,128)}, f32[8,64,64]{2,1,0:T(8,128)}, f32[8]{0:T(128)}, f32[8,1024]{1,0:T(8,128)}, bf16[8,512]{1,0:T(8,128)(2,1)}) custom-call(f32[8,64]{1,0:T(8,128)} %get-tuple-element.10.refs_0_, f32[8,64,64]{2,1,0:T(8,128)} %get-tuple-element.11.refs_1_, f32[8]{0:T(128)} %get-tuple-element.12.refs_2_, ...), custom_call_target="tpu_custom_call" | custom-call | tf_op jit(solution)/shard_map/hand_over/pallas_call | solution.py:496
